TPU v7x, 32 devices: a whole 2x2x4 slice. The times are simulated.
32 devices in a mesh: groups: 2 (over x), row: 2 (over core), col: 8 (over z, y).
Axes of the slice: x: 2, y: 2, z: 4, core: 2. Of those that a mesh axis runs over, the one named last changes fastest.
Arguments:
- pair: bfloat16 [1280, 640, 128], P(('groups', 'col'), 'row'), parts along dimension 0, may hold values from -6 to 6
- token_mask: int32 [1280], P('groups'), parts along dimension 0, may hold values 0 or 1
- start_gain: float32 [128], replicated, may hold values from 0.25 to 1.75
- start_head_gain: float32 [128], replicated, may hold values from 0.25 to 1.75
- start_in: bfloat16 [128, 512], replicated, may hold values from -0.5 to 0.5
- start_out: bfloat16 [128, 128], replicated, may hold values from -0.5 to 0.5
- end_gain: float32 [128], replicated, may hold values from 0.25 to 1.75
- end_head_gain: float32 [128], replicated, may hold values from 0.25 to 1.75
- end_in: bfloat16 [128, 512], replicated, may hold values from -0.5 to 0.5
- end_out: bfloat16 [128, 128], replicated, may hold values from -0.5 to 0.5
- trans_gain: float32 [128], replicated, may hold values from 0.25 to 1.75
- trans_in: bfloat16 [128, 1024], replicated, may hold values from -0.5 to 0.5
- trans_out: bfloat16 [512, 128], replicated, may hold values from -0.25 to 0.25
Outputs:
- update_start: bfloat16 [1280, 640, 128], P(('groups', 'col'), 'row'), parts along dimension 0
- update_end: bfloat16 [1280, 640, 128], P(('groups', 'col'), 'row'), parts along dimension 0
- update_trans: bfloat16 [1280, 640, 128], P(('groups', 'col'), 'row'), parts along dimension 0
There are 2 independent parts, one for each index of `groups`. A program takes and returns all parts, laid end to end along the dimension named above; an argument that names none is the same for every part. Nothing has to cross between parts.
Inputs may be any that keep to these rules, and one draw needn't show every extreme that they name: `token_mask`: 1 marks a valid token of the complex, 0 a padded one.
All inputs are finite; a program needn't handle non-finite values.
Results may differ from a plain program's by a relative error of at most 0.018.
Values may be sent and summed in bfloat16 or wider, within the bound.
A program may use at most 192 MiB of HBM per device.

v0:
```python
import math

import jax
import jax.numpy as jnp
from jax import lax
from jax.sharding import PartitionSpec as P

HEADS = 4


EPSILON = 1e-05


def layer_norm(values, scales):
    average = jnp.mean(values, axis=-1, keepdims=True)
    centered = values - average
    variance = jnp.mean(centered * centered, axis=-1, keepdims=True)
    return centered * lax.rsqrt(variance + EPSILON) * scales


def feature(values):
    return jax.nn.elu(values) + 1.0


def key_value(project, pair_valid, width, depth):
    shape = project.shape[:2] + (HEADS, depth)
    key_feat = (
        (feature(project[..., :width]) * pair_valid[..., None]).astype(jnp.bfloat16).reshape(shape)
    )
    values = project[..., width : 2 * width].astype(jnp.bfloat16).reshape(shape)
    return (key_feat, values)


def finish(queries, gating, state, totals, numer_form, denom_form, head_gain, w_out):
    width = gating.shape[-1]
    query_f = queries.astype(jnp.float32)
    numer = jnp.einsum(numer_form, query_f, state)
    denom = jnp.maximum(jnp.einsum(denom_form, query_f, totals), 1.0)
    attended = (numer / denom[..., None]).reshape(gating.shape)
    scaled = attended * lax.rsqrt(jnp.mean(attended * attended, axis=-1, keepdims=True) + EPSILON)
    scaled = (scaled * head_gain * gating).astype(jnp.bfloat16)
    update = jnp.dot(scaled.reshape(-1, width), w_out, preferred_element_type=jnp.float32)
    return update.astype(jnp.bfloat16).reshape(gating.shape)


def shards(
    pair,
    token_mask,
    start_gain,
    start_head_gain,
    start_in,
    start_out,
    end_gain,
    end_head_gain,
    end_in,
    end_out,
    trans_gain,
    trans_in,
    trans_out,
):
    row_count = pair.shape[0]
    col_count = pair.shape[1]
    width = pair.shape[2]
    depth = width // HEADS
    valid = token_mask.astype(jnp.float32)
    row_valid = lax.dynamic_slice_in_dim(valid, lax.axis_index("col") * row_count, row_count)
    col_valid = lax.dynamic_slice_in_dim(valid, lax.axis_index("row") * col_count, col_count)
    pair_valid = row_valid[:, None] * col_valid[None, :]
    head_shape = (row_count, col_count, HEADS, depth)
    anchor = pair.astype(jnp.float32)
    normed = layer_norm(anchor, start_gain).astype(jnp.bfloat16)
    project = jnp.dot(normed.reshape(-1, width), start_in, preferred_element_type=jnp.float32)
    project = project.reshape(row_count, col_count, 4 * width)
    queries = feature(project[..., :width]).astype(jnp.bfloat16).reshape(head_shape)
    key_feat, values = key_value(project[..., width : 3 * width], pair_valid, width, depth)
    gating = jax.nn.sigmoid(project[..., 3 * width :])
    partial_value = jnp.einsum(
        "ijhd,ijhe->ihde", key_feat, values, preferred_element_type=jnp.float32
    )
    key_part = jnp.sum(key_feat, axis=1, dtype=jnp.float32)
    state, totals = (
        lax.psum(partial_value.astype(jnp.bfloat16), "row").astype(jnp.float32),
        lax.psum(key_part.astype(jnp.bfloat16), "row").astype(jnp.float32),
    )
    update_start = finish(
        queries,
        gating,
        state,
        totals,
        "ijhd,ihde->ijhe",
        "ijhd,ihd->ijh",
        start_head_gain,
        start_out,
    )
    first_sum = anchor + update_start.astype(jnp.float32)
    normed = layer_norm(first_sum, end_gain).astype(jnp.bfloat16)
    project = jnp.dot(normed.reshape(-1, width), end_in, preferred_element_type=jnp.float32)
    project = project.reshape(row_count, col_count, 4 * width)
    key_feat, values = key_value(project[..., width : 3 * width], pair_valid, width, depth)
    partial_value = jnp.einsum(
        "ijhd,ijhe->jhde", key_feat, values, preferred_element_type=jnp.float32
    )
    key_part = jnp.sum(key_feat, axis=0, dtype=jnp.float32)
    queries = feature(project[..., :width]).astype(jnp.bfloat16).reshape(head_shape)
    gating = jax.nn.sigmoid(project[..., 3 * width :])
    state, totals = (
        lax.psum(partial_value.astype(jnp.bfloat16), "col").astype(jnp.float32),
        lax.psum(key_part.astype(jnp.bfloat16), "col").astype(jnp.float32),
    )
    update_end = finish(
        queries, gating, state, totals, "ijhd,jhde->ijhe", "ijhd,jhd->ijh", end_head_gain, end_out
    )
    second_sum = first_sum + update_end.astype(jnp.float32)
    hidden_width = trans_out.shape[0]
    row_block = math.gcd(row_count, 8)

    def transition(block):
        normed_block = layer_norm(block, trans_gain).astype(jnp.bfloat16)
        lifted = jnp.dot(normed_block, trans_in, preferred_element_type=jnp.float32)
        hidden = (jax.nn.silu(lifted[:, :hidden_width]) * lifted[:, hidden_width:]).astype(
            jnp.bfloat16
        )
        return jnp.dot(hidden, trans_out, preferred_element_type=jnp.float32).astype(jnp.bfloat16)

    update_trans = lax.map(
        transition, second_sum.reshape(row_count // row_block, row_block * col_count, width)
    )
    update_trans = update_trans.reshape(row_count, col_count, width)
    return (update_start, update_end, update_trans)


def solution(mesh):
    in_specs = (
        P(("groups", "col"), "row", None),
        P("groups"),
        P(),
        P(),
        P(),
        P(),
        P(),
        P(),
        P(),
        P(),
        P(),
        P(),
        P(),
    )
    out_specs = (
        P(("groups", "col"), "row", None),
        P(("groups", "col"), "row", None),
        P(("groups", "col"), "row", None),
    )
    return jax.shard_map(shards, mesh=mesh, in_specs=in_specs, out_specs=out_specs, check_vma=False)
```

profile of v0, /device:TPU:0, one launch (start us, length us, event | category | flops | bytes accessed | tf_op | source)
XLA Modules:
  0.0 754.1 jit_solution(8597856424074216572)
XLA Ops:
  8.1 5.2 convert_reduce_fusion
  13.3 8.5 %fusion.12 = f32[80,320]{1,0:T(8,128)S(1)} fusion(bf16[80,320,128]{2,1,0:T(8,128)(2,1)S(1)} %copy-done.2, f32[80,320]{1,0:T(8,128)S(1)} %broadcast_multiply_fusion.3), kind=kLoop, calls=%fused_computation.36 | loop fusion | flops 13081600 | bytes 6758400 | tf_op jit(solution)/shard_map/reduce_sum | solution.py:17
  22.0 18.3 %fusion.41 = f32[80,320,512]{2,1,0:T(8,128)} fusion(bf16[80,320,128]{2,1,0:T(8,128)(2,1)S(1)} %copy-done.2, f32[128]{0:T(128)S(1)} %copy-done.9, f32[80,320]{1,0:T(8,128)S(1)} %add_rsqrt_fusion.4, f32[80,320]{1,0:T(8,128)S(1)} %broadcast_multiply_fusion.3, bf16[128,512]{1,0:T(8,128)(2,1)S(1)} %copy-done), kind=kOutput, calls=%fused_computation.73 | convolution fusion | flops 3371827200 | bytes 59318784 | tf_op jit(solution)/shard_map/dot_general | solution.py:72
  40.2 17.5 %fusion.54 = (bf16[80,128]{1,0:T(8,128)(2,1)S(1)}, bf16[80,320,128]{2,1,0:T(8,128)(2,1)}, bf16[80,320,128]{2,1,0:T(8,128)(2,1)}) fusion(f32[80,320]{1,0:T(8,128)S(1)} %broadcast_multiply_fusion.1, f32[80,320,512]{2,1,0:T(8,128)} %fusion.41), kind=kLoop, calls=%fused_computation.94 | loop fusion | flops 22927360 | bytes 32890880 | tf_op jit(solution)/shard_map/reduce_sum | solution.py:80
  57.7 9.8 %copy.52 = bf16[80,320,128]{1,2,0:T(8,128)(2,1)} copy(bf16[80,320,128]{2,1,0:T(8,128)(2,1)} %get-tuple-element.53) | data formatting | bytes 13107200 | tf_op jit(solution)/shard_map/convert_element_type | solution.py:28
  67.5 9.8 %copy.53 = bf16[80,320,128]{1,2,0:T(8,128)(2,1)} copy(bf16[80,320,128]{2,1,0:T(8,128)(2,1)} %get-tuple-element.55) | data formatting | bytes 13107200 | tf_op jit(solution)/shard_map/slice | solution.py:30
  77.3 9.8 %convolution_convert_fusion.4 = bf16[80,4,32,32]{3,2,1,0:T(8,128)(2,1)} fusion(bf16[80,320,4,32]{1,3,2,0:T(8,128)(2,1)} %bitcast.96, bf16[80,320,4,32]{1,3,2,0:T(8,128)(2,1)} %bitcast.97), kind=kOutput, calls=%fused_computation.80 | convolution fusion | flops 210042880 | bytes 13762560 | tf_op jit(solution)/shard_map/ijhd,ijhe->ihde/dot_general | solution.py:77
  87.7 13.2 %fusion.21 = bf16[80,320,128]{2,1,0:T(8,128)(2,1)} fusion(f32[80,320,512]{2,1,0:T(8,128)} %fusion.41), kind=kLoop, calls=%fused_computation.45 | loop fusion | flops 16384000 | bytes 19660800 | tf_op jit(solution)/shard_map/convert_element_type | solution.py:74
  101.0 3.9 psum.29
  105.0 10.4 %copy.54 = bf16[80,320,128]{1,2,0:T(8,128)(2,1)} copy(bf16[80,320,128]{2,1,0:T(8,128)(2,1)} %fusion.21) | data formatting | bytes 13107200 | tf_op jit(solution)/shard_map/convert_element_type | solution.py:74
  115.5 4.7 fusion.56
  120.3 12.1 %multiply_reduce_fusion.2 = (f32[80,320]{1,0:T(8,128)S(1)}, f32[80,320,4,32]{1,3,2,0:T(8,128)}) fusion(f32[80,320,4]{1,2,0:T(4,128)S(1)} %fusion.49, bf16[80,4,32,32]{3,2,1,0:T(8,128)(2,1)} %all-reduce.4.cloned.1.call-done, bf16[80,320,4,32]{1,3,2,0:T(8,128)(2,1)} %bitcast.95), kind=kOutput, calls=%fused_computation.33 | convolution fusion | flops 219520000 | bytes 20828160 | tf_op jit(solution)/shard_map/ijhd,ihde->ijhe/dot_general | solution.py:37
  132.4 14.9 %copy.57 = f32[80,320,128]{2,1,0:T(8,128)} copy(f32[80,320,128]{1,2,0:T(8,128)} %bitcast.103) | data formatting | bytes 26214400 | tf_op jit(solution)/shard_map/reshape | solution.py:39
  147.4 9.5 %fusion.37 = bf16[80,320,128]{2,1,0:T(8,128)(2,1)S(1)} fusion(f32[80,320,512]{2,1,0:T(8,128)} %fusion.41, f32[80,320,128]{2,1,0:T(8,128)} %copy.57, f32[128]{0:T(128)S(1)} %copy-done.11, f32[80,320]{1,0:T(8,128)S(1)} %add_rsqrt_fusion.3), kind=kLoop, calls=%fused_computation.68 | loop fusion | flops 22937600 | bytes 32870912 | tf_op jit(solution)/shard_map/convert_element_type | solution.py:41
  156.8 3.8 convolution_convert_fusion.2
  160.6 9.0 %fusion.39 = f32[80,320]{1,0:T(8,128)S(1)} fusion(bf16[80,320,128]{2,1,0:T(8,128)(2,1)} %bitcast.84, bf16[80,320,128]{2,1,0:T(8,128)(2,1)} %param.15), kind=kLoop, calls=%fused_computation.70 | loop fusion | flops 13081600 | bytes 13209600 | tf_op jit(solution)/shard_map/reduce_sum | solution.py:15
  169.7 10.1 %multiply_reduce_fusion.3 = f32[80,320]{1,0:T(8,128)S(1)} fusion(bf16[80,320,128]{2,1,0:T(8,128)(2,1)} %bitcast.85, bf16[80,320,128]{2,1,0:T(8,128)(2,1)} %param.15, f32[80,320]{1,0:T(8,128)S(1)} %broadcast_multiply_fusion.2), kind=kLoop, calls=%fused_computation.67 | loop fusion | flops 19635200 | bytes 13312000 | tf_op jit(solution)/shard_map/reduce_sum | solution.py:17
  179.9 20.7 %fusion.40 = f32[80,320,512]{2,1,0:T(8,128)} fusion(bf16[80,320,128]{2,1,0:T(8,128)(2,1)} %bitcast.86, bf16[80,320,128]{2,1,0:T(8,128)(2,1)S(1)} %bitcast.81, f32[128]{0:T(128)S(1)} %copy-done.10, f32[80,320]{1,0:T(8,128)S(1)} %add_rsqrt_fusion.2, f32[80,320]{1,0:T(8,128)S(1)} %broadcast_multiply_fusion.2, bf16[128,512]{1,0:T(8,128)(2,1)S(1)} %copy-done.5), kind=kOutput, calls=%fused_computation.72 | convolution fusion | flops 3378380800 | bytes 65872384 | tf_op jit(solution)/shard_map/dot_general | solution.py:97
  200.6 17.8 %fusion.52 = (bf16[320,128]{1,0:T(8,128)(2,1)S(1)}, bf16[80,320,128]{2,1,0:T(8,128)(2,1)}, bf16[80,320,128]{2,1,0:T(8,128)(2,1)}) fusion(f32[80,320]{1,0:T(8,128)S(1)} %broadcast_multiply_fusion.1, f32[80,320,512]{2,1,0:T(8,128)} %fusion.40), kind=kLoop, calls=%fused_computation.93 | loop fusion | flops 22896640 | bytes 32952320 | tf_op jit(solution)/shard_map/reduce_sum | solution.py:103
  218.4 12.8 %copy.75 = bf16[80,320,128]{0,2,1:T(8,128)(2,1)} copy(bf16[80,320,128]{2,1,0:T(8,128)(2,1)} %get-tuple-element.51) | data formatting | bytes 13107200 | tf_op jit(solution)/shard_map/reshape | solution.py:28
  231.2 12.8 %copy.76 = bf16[80,320,128]{0,2,1:T(8,128)(2,1)} copy(bf16[80,320,128]{2,1,0:T(8,128)(2,1)} %get-tuple-element.54) | data formatting | bytes 13107200 | tf_op jit(solution)/shard_map/reshape | solution.py:30
  244.7 12.2 %convolution_convert_fusion.3 = bf16[320,4,32,32]{3,2,1,0:T(8,128)(2,1)} fusion(bf16[80,320,4,32]{0,3,2,1:T(8,128)(2,1)} %bitcast.92, bf16[80,320,4,32]{0,3,2,1:T(8,128)(2,1)} %bitcast.93), kind=kOutput, calls=%fused_computation.71 | convolution fusion | flops 211025920 | bytes 15728640 | tf_op jit(solution)/shard_map/ijhd,ijhe->jhde/dot_general | solution.py:100
  256.9 13.2 %fusion.28 = bf16[80,320,128]{2,1,0:T(8,128)(2,1)} fusion(f32[80,320,512]{2,1,0:T(8,128)} %fusion.40), kind=kLoop, calls=%fused_computation.52 | loop fusion | flops 16384000 | bytes 19660800 | tf_op jit(solution)/shard_map/convert_element_type | solution.py:104
  270.2 13.1 %copy.77 = bf16[80,320,128]{0,2,1:T(8,128)(2,1)} copy(bf16[80,320,128]{2,1,0:T(8,128)(2,1)} %fusion.28) | data formatting | bytes 13107200 | tf_op jit(solution)/shard_map/reshape | solution.py:104
  283.3 306.6 %all-reduce.6.cloned.1.call-done = (bf16[320,4,32]{0,2,1:T(8,128)(2,1)}, bf16[320,4,32,32]{3,2,1,0:T(8,128)(2,1)}) async-done(((bf16[320,4,32]{0,2,1:T(8,128)(2,1)}, bf16[320,4,32,32]{3,2,1,0:T(8,128)(2,1)}), (bf16[320,4,32]{0,2,1:T(8,128)(2,1)}, bf16[320,4,32,32]{3,2,1,0:T(8,128)(2,1)})) %all-reduce.6.cloned.1.call-update) | async-done | bytes 2703376 | tf_op jit(solution)/shard_map/psum | solution.py:108
  591.3 5.5 fusion.57
  596.9 13.9 %multiply_reduce_fusion.1 = (f32[80,320]{0,1:T(8,128)S(1)}, f32[80,320,4,32]{0,3,2,1:T(8,128)}) fusion(f32[80,320,4]{0,2,1:T(4,128)S(1)} %maximum_bitcast_fusion, bf16[320,4,32,32]{3,2,1,0:T(8,128)(2,1)} %get-tuple-element.49, bf16[80,320,4,32]{0,3,2,1:T(8,128)(2,1)} %bitcast.105), kind=kOutput, calls=%fused_computation.28 | convolution fusion | flops 219520000 | bytes 22794240 | tf_op jit(solution)/shard_map/ijhd,jhde->ijhe/dot_general | solution.py:37
  610.9 18.9 %copy.68 = f32[80,320,128]{2,1,0:T(8,128)} copy(f32[80,320,128]{0,2,1:T(8,128)} %bitcast.102) | data formatting | bytes 26214400 | tf_op jit(solution)/shard_map/reshape | solution.py:39
  629.9 9.6 %fusion.38 = bf16[80,320,128]{2,1,0:T(8,128)(2,1)S(1)} fusion(f32[80,320,512]{2,1,0:T(8,128)} %fusion.40, f32[80,320,128]{2,1,0:T(8,128)} %copy.68, f32[128]{0:T(128)S(1)} %copy-done.12, f32[80,320]{1,0:T(8,128)S(1)} %add_rsqrt_fusion.1), kind=kLoop, calls=%fused_computation.69 | loop fusion | flops 22937600 | bytes 32870912 | tf_op jit(solution)/shard_map/convert_element_type | solution.py:41
  642.5 6.4 convert_add_fusion.1
  648.9 97.0 %while.10 = (s32[]{:T(128)}, bf16[10,2560,128]{2,1,0:T(8,128)(2,1)}, f32[10,2560,128]{2,1,0:T(8,128)}, f32[128]{0:T(128)S(1)}, bf16[128,1024]{1,0:T(8,128)(2,1)S(1)}, /*index=5*/bf16[512,128]{1,0:T(8,128)(2,1)S(1)}, s32[]{:T(128)}) while((s32[]{:T(128)}, bf16[10,2560,128]{2,1,0:T(8,128)(2,1)}, f32[10,2560,128]{2,1,0:T(8,128)}, ...), condition=%wide.region_15.16_spmd, body=%wide.region_12.15_spmd.sunk | while | flops 1017448960 | bytes 26046036 | solution.py:125
  652.8 3.4 fusion.84
  656.2 2.4 fusion.85
  662.5 3.4 fusion.84
  665.9 2.4 fusion.85
  672.2 3.4 fusion.84
  675.6 2.4 fusion.85
  681.9 3.4 fusion.84
  685.3 2.4 fusion.85
  691.6 3.4 fusion.84
  695.0 2.4 fusion.85
  701.3 3.4 fusion.84
  711.0 3.4 fusion.84
  714.4 2.4 fusion.85
  720.7 3.4 fusion.84
  730.4 3.4 fusion.84
  740.1 3.4 fusion.84
  743.5 2.4 fusion.85
  (110 shorter events, 53.7 us)
Async XLA Ops:
  7.2 14.8 %copy-start = (bf16[128,512]{1,0:T(8,128)(2,1)S(1)}, bf16[128,512]{1,0:T(8,128)(2,1)}, u32[]{:S(2)}) copy-start(bf16[128,512]{1,0:T(8,128)(2,1)} %param.19) | copy-start | bytes 393220
  7.2 14.8 %copy-start.9 = (f32[128]{0:T(128)S(1)}, f32[128]{0:T(128)}, u32[]{:S(2)}) copy-start(f32[128]{0:T(128)} %param.17) | copy-start | bytes 1540
  7.2 113.1 %all-reduce.4.cloned.1.call-start = ((), (), s32[]{:S(2)}) async-start(), calls=%async_computation | async-start | bytes 5242880 | tf_op jit(solution)/shard_map/psum | solution.py:82
  8.0 5.3 copy-start.2
  87.2 502.7 %all-reduce.6.cloned.1.call-start = ((), (), s32[]{:S(2)}) async-start(), calls=%async_computation.1 | async-start | bytes 21168128 | tf_op jit(solution)/shard_map/psum | solution.py:108
  132.4 14.9 %copy-start.11 = (f32[128]{0:T(128)S(1)}, f32[128]{0:T(128)}, u32[]{:S(2)}) copy-start(f32[128]{0:T(128)} %param.18) | copy-start | bytes 1540
  147.3 9.5 %copy-start.7 = (bf16[128,128]{1,0:T(8,128)(2,1)S(1)}, bf16[128,128]{1,0:T(8,128)(2,1)}, u32[]{:S(2)}) copy-start(bf16[128,128]{1,0:T(8,128)(2,1)} %param.20) | copy-start | bytes 98308
  160.6 19.2 %slice-start = ((s8[6553600]{0:T(1024)(128)(4,1)}), s8[2359296]{0:T(1024)(128)(4,1)S(1)}, s32[]{:S(2)}) async-start(s8[6553600]{0:T(1024)(128)(4,1)} %bitcast.80), calls=%async_computation.2 | async-start | bytes 4718592
  160.6 19.2 %copy-start.5 = (bf16[128,512]{1,0:T(8,128)(2,1)S(1)}, bf16[128,512]{1,0:T(8,128)(2,1)}, u32[]{:S(2)}) copy-start(bf16[128,512]{1,0:T(8,128)(2,1)} %param.23) | copy-start | bytes 393220
  160.6 19.2 %copy-start.10 = (f32[128]{0:T(128)S(1)}, f32[128]{0:T(128)}, u32[]{:S(2)}) copy-start(f32[128]{0:T(128)} %param.21) | copy-start | bytes 1540
  169.7 10.2 %slice-start.1 = ((s8[6553600]{0:T(1024)(128)(4,1)}), s8[4194304]{0:T(1024)(128)(4,1)S(1)}, s32[]{:S(2)}) async-start(s8[6553600]{0:T(1024)(128)(4,1)} %bitcast.80), calls=%async_computation.3 | async-start | bytes 8388608
  610.9 19.0 %copy-start.12 = (f32[128]{0:T(128)S(1)}, f32[128]{0:T(128)}, u32[]{:S(2)}) copy-start(f32[128]{0:T(128)} %param.22) | copy-start | bytes 1540
  610.9 30.8 %slice-start.4 = ((s8[6553600]{0:T(1024)(128)(4,1)}), s8[2359296]{0:T(1024)(128)(4,1)S(1)}, s32[]{:S(2)}) async-start(s8[6553600]{0:T(1024)(128)(4,1)} %bitcast.88), calls=%async_computation.6 | async-start | bytes 4718592
  629.9 9.7 %copy-start.8 = (bf16[128,128]{1,0:T(8,128)(2,1)S(1)}, bf16[128,128]{1,0:T(8,128)(2,1)}, u32[]{:S(2)}) copy-start(bf16[128,128]{1,0:T(8,128)(2,1)} %param.24) | copy-start | bytes 98308
  629.9 11.7 %slice-start.5 = ((s8[6553600]{0:T(1024)(128)(4,1)}), s8[4194304]{0:T(1024)(128)(4,1)S(1)}, s32[]{:S(2)}) async-start(s8[6553600]{0:T(1024)(128)(4,1)} %bitcast.88), calls=%async_computation.7 | async-start | bytes 8388608
  639.5 2.2 slice-start.2
  639.6 2.9 slice-start.3
  641.6 7.3 copy-start.3
  642.5 6.5 copy-start.4
  642.5 6.5 copy-start.6
  642.5 6.5 copy-start.13
  745.9 0.9 copy-start.1
Sparse Core Ops, SparseCore 0:
  87.3 24.8 all-reduce.3
  257.1 332.7 all-reduce.5
where the time goes:
time: 764 us; the launch traced here: 754 us
  waiting for transfers between devices  307 us (40%)
  matrix products  162 us (21%)
  other arithmetic  159 us (21%)
  local copies, waits for them, and re-layouts  107 us (14%)
  between operations  14.9 us (2%)
    psum x1, waiting for transfers between devices, shards(): lax.psum(key_part.astype(jnp.bfloat16), 'col').astype(jnp.float32)  307 us
    reduce_sum x12, other arithmetic, layer_norm(): variance = jnp.mean(centered * centered, axis=-1, keepdims=True)  39.5 us
    dot_general x10, matrix products, transition(): lifted = jnp.dot(normed_block, trans_in, preferred_element_type=jnp.float32)  34.3 us
    reshape x2, local copies, waits for them, and re-layouts, finish(): attended = (numer / denom[..., None]).reshape(gating.shape)  33.7 us
    reduce_sum x12, other arithmetic, layer_norm(): average = jnp.mean(values, axis=-1, keepdims=True)  31.5 us
    convert_element_type x2, other arithmetic, shards(): feature(project[..., :width]).astype(jnp.bfloat16).reshape(head_shape)  26.5 us
    dot_general x2, matrix products, finish(): numer = jnp.einsum(numer_form, query_f, state)  26 us
    dot_general x10, matrix products, transition(): jnp.dot(hidden, trans_out, preferred_element_type=jnp.float32)  24.2 us
  transfers between devices with their start and end apart: 2, of which 1 were waited for; matrix products, arithmetic and copies ran while one was open for 7% of the time, Pallas kernels for 0%

commit v1 on v0

v1 whole, which is shorter than its diff:
```python
import functools
import math

import jax
import jax.numpy as jnp
from jax import lax
from jax.experimental import pallas as pl
from jax.experimental.pallas import tpu as pltpu
from jax.sharding import PartitionSpec as P

HEADS = 4
EPSILON = 1e-05
F32 = jnp.float32
BF16 = jnp.bfloat16
CHUNKS = 2
VMEM_BYTES = 52 * 1024 * 1024


def layer_norm(values, scales):
    average = jnp.mean(values, axis=-1, keepdims=True)
    centered = values - average
    variance = jnp.mean(centered * centered, axis=-1, keepdims=True)
    return centered * lax.rsqrt(variance + EPSILON) * scales


def feature(values):
    return jnp.maximum(values + 1.0, jnp.exp(jnp.minimum(values, 0.0)))


def sigmoid(values):
    return 0.5 + 0.5 * jnp.tanh(0.5 * values)


def matmul(left, right):
    return jnp.dot(left, right, preferred_element_type=F32)


def same_head(width):
    depth = width // HEADS
    rows = lax.broadcasted_iota(jnp.int32, (width, width), 0) // depth
    cols = lax.broadcasted_iota(jnp.int32, (width, width), 1) // depth
    return rows == cols


def outer_compact(keys, values):
    width = keys.shape[-1]
    depth = width // HEADS
    full = lax.dot_general(keys, values, (((0,), (0,)), ((), ())), preferred_element_type=F32)
    head = lax.broadcasted_iota(jnp.int32, (depth, width), 1) // depth
    result = full[:depth]
    for h in range(1, HEADS):
        result = jnp.where(head == h, full[h * depth : (h + 1) * depth], result)
    return result


def expand(state, same):
    tiled = jnp.concatenate([state.astype(F32)] * HEADS, axis=0)
    return jnp.where(same, tiled, 0.0).astype(BF16)


def query_gate(w):
    width = w.shape[0]
    return jnp.concatenate([w[:, :width], w[:, 3 * width :]], axis=1)


def head_norm(numer, denom, gate, head_gain):
    attended = numer / jnp.maximum(denom, 1.0)
    scale = lax.rsqrt(jnp.mean(attended * attended, axis=-1, keepdims=True) + EPSILON)
    return (attended * scale * head_gain * sigmoid(gate)).astype(BF16)


def row_state_kernel(row_valid, pair, col_mask, gain, w, out):
    count, _, width = pair.shape
    depth = width // HEADS
    base = pl.program_id(0) * count
    w_kv = w[:, width : 3 * width]
    mask = col_mask[...]
    scales = gain[...]

    def one(i):
        normed = layer_norm(pair[i].astype(F32), scales).astype(BF16)
        project = matmul(normed, w_kv)
        keys = (feature(project[:, :width]) * mask).astype(BF16)
        values = project[:, width:].astype(BF16)
        valid = row_valid[base + i]
        out[i, 0:depth, :] = (outer_compact(keys, values) * valid).astype(BF16)
        total = jnp.sum(keys.astype(F32), axis=0, keepdims=True) * valid
        out[i, depth : depth + 16, :] = jnp.broadcast_to(total, (16, width)).astype(BF16)

    def body(step, carry):
        one(2 * step)
        one(2 * step + 1)
        return carry

    lax.fori_loop(0, count // 2, body, 0)


def start_kernel(pair, state, gain, head_gain, w, w_out, end_gain, *rest):
    update, normed_end = rest[-2:]
    count, _, width = pair.shape
    depth = width // HEADS
    same = same_head(width)
    ones = same.astype(F32).astype(BF16)
    w_qg = query_gate(w[...])

    def one(i):
        field = pair[i].astype(F32)
        normed = layer_norm(field, gain[...]).astype(BF16)
        project = matmul(normed, w_qg)
        queries = feature(project[:, :width]).astype(BF16)
        totals = state[i, depth : depth + 16, :].astype(F32)[0:1]
        numer = matmul(queries, expand(state[i, 0:depth, :], same))
        denom = matmul((queries.astype(F32) * totals).astype(BF16), ones)
        scaled = head_norm(numer, denom, project[:, width:], head_gain[...])
        result = matmul(scaled, w_out[...]).astype(BF16)
        update[i] = result
        normed_end[i] = layer_norm(field + result.astype(F32), end_gain[...]).astype(BF16)

    def body(step, carry):
        one(2 * step)
        one(2 * step + 1)
        return carry

    lax.fori_loop(0, count // 2, body, 0)


def columns_first(normed, scratch):
    rows, count, width = normed.shape
    scratch[...] = normed[...].astype(F32).reshape(rows * count, width)
    return jnp.concatenate(
        [scratch[pl.ds(j, rows, stride=count), :] for j in range(count)], axis=0
    ).astype(BF16)


def column_state_kernel(first, col_valid, normed, row_mask, w, out, scratch):
    rows, count, width = normed.shape
    depth = width // HEADS
    base = first + pl.program_id(0) * count
    project = matmul(columns_first(normed, scratch), w[:, width : 3 * width])
    keys = feature(project[:, :width]).reshape(count, rows, width) * row_mask[...][None]
    keys = keys.astype(BF16)
    values = project[:, width:].reshape(count, rows, width).astype(BF16)
    totals = []
    for j in range(count):
        valid = col_valid[base + j]
        out[0, j * depth : (j + 1) * depth, :] = (
            outer_compact(keys[j], values[j]) * valid
        ).astype(BF16)
        totals.append(jnp.sum(keys[j].astype(F32), axis=0, keepdims=True) * valid)
    out[0, count * depth : count * (depth + 1), :] = jnp.concatenate(totals, axis=0).astype(BF16)
    left = out.shape[1] - count * (depth + 1)
    if left:
        out[0, count * (depth + 1) :, :] = jnp.zeros((left, width), BF16)


def end_kernel(
    normed, pair, update_start, state, head_gain, w, w_out, trans_gain, trans_in, trans_out, *rest
):
    update_end, update_trans, scratch, turned = rest[-4:]
    rows, count, width = normed.shape
    depth = width // HEADS
    hidden = trans_out.shape[0]
    same = same_head(width)
    ones = same.astype(F32).astype(BF16)
    project = matmul(columns_first(normed, scratch), query_gate(w[...]))
    queries = feature(project[:, :width]).reshape(count, rows, width).astype(BF16)
    totals = state[0, count * depth : count * (depth + 1), :].astype(F32)
    numer, weighted = [], []
    for j in range(count):
        numer.append(matmul(queries[j], expand(state[0, j * depth : (j + 1) * depth, :], same)))
        weighted.append(queries[j].astype(F32) * totals[j : j + 1])
    denom = matmul(jnp.concatenate(weighted, axis=0).astype(BF16), ones)
    scaled = head_norm(
        jnp.concatenate(numer, axis=0), denom, project[:, width:], head_gain[...]
    )
    result = matmul(scaled, w_out[...])
    for j in range(count):
        turned[pl.ds(j, rows, stride=count), :] = result[j * rows : (j + 1) * rows]
    stride = math.gcd(rows, 16)

    def body(step, carry):
        at = pl.ds(step * stride, stride)
        flat = pl.ds(pl.multiple_of(step * stride * count, stride * count), stride * count)
        ended = turned[flat, :].astype(BF16)
        update_end[at] = ended.reshape(stride, count, width)
        field = pair[at].astype(F32) + update_start[at].astype(F32)
        field = field.reshape(stride * count, width) + ended.astype(F32)
        y = layer_norm(field, trans_gain[...]).astype(BF16)
        lifted = matmul(y, trans_in[...])
        gate = 0.5 * lifted[:, :hidden]
        h = ((gate + gate * jnp.tanh(gate)) * lifted[:, hidden:]).astype(BF16)
        moved = matmul(h, trans_out[...]).astype(BF16)
        update_trans[at] = moved.reshape(stride, count, width)
        return carry

    lax.fori_loop(0, rows // stride, body, 0)


def exchange_sum(values, size, bits):
    me = lax.axis_index("col")
    for bit in bits:
        half = values.shape[0] // 2
        mine = (me >> bit) & 1
        pairs = [(d, d ^ (1 << bit)) for d in range(size)]
        sent = lax.dynamic_slice_in_dim(values, (1 - mine) * half, half)
        kept = lax.dynamic_slice_in_dim(values, mine * half, half)
        got = lax.ppermute(sent, "col", pairs)
        values = (kept.astype(F32) + got.astype(F32)).astype(BF16)
    for bit in reversed(bits):
        mine = (me >> bit) & 1
        pairs = [(d, d ^ (1 << bit)) for d in range(size)]
        got = lax.ppermute(values, "col", pairs)
        values = jnp.where(
            mine == 1,
            jnp.concatenate([got, values], axis=0),
            jnp.concatenate([values, got], axis=0),
        )
    return values


def params():
    return pltpu.CompilerParams(vmem_limit_bytes=VMEM_BYTES, dimension_semantics=("arbitrary",))


def cost(flops):
    return pl.CostEstimate(flops=int(flops), bytes_accessed=1 << 20, transcendentals=0)


def shards(
    size,
    pair,
    token_mask,
    start_gain,
    start_head_gain,
    start_in,
    start_out,
    end_gain,
    end_head_gain,
    end_in,
    end_out,
    trans_gain,
    trans_in,
    trans_out,
):
    rows, cols, width = pair.shape
    depth = width // HEADS
    valid = token_mask.astype(F32)
    row_valid = lax.dynamic_slice_in_dim(valid, lax.axis_index("col") * rows, rows)
    col_valid = lax.dynamic_slice_in_dim(valid, lax.axis_index("row") * cols, cols)
    row_mask = jnp.broadcast_to(row_valid[:, None], (rows, width))
    col_mask = jnp.broadcast_to(col_valid[:, None], (cols, width))
    gains = [
        g.reshape(1, width) for g in (start_gain, start_head_gain, end_gain, end_head_gain, trans_gain)
    ]
    start_gain, start_head_gain, end_gain, end_head_gain, trans_gain = gains
    smem = pl.BlockSpec(memory_space=pltpu.SMEM)
    anywhere = pl.BlockSpec(memory_space=pl.ANY)

    def whole(array):
        return pl.BlockSpec(array.shape, lambda g: (0,) * array.ndim)

    group = math.gcd(rows, 8)
    packed = depth + 16
    row_state = pl.pallas_call(
        row_state_kernel,
        grid=(rows // group,),
        in_specs=[
            smem,
            pl.BlockSpec((group, cols, width), lambda g: (g, 0, 0)),
            whole(col_mask),
            whole(start_gain),
            whole(start_in),
        ],
        out_specs=pl.BlockSpec((group, packed, width), lambda g: (g, 0, 0)),
        out_shape=jax.ShapeDtypeStruct((rows, packed, width), BF16),
        compiler_params=params(),
        cost_estimate=cost(2e10),
        name="row_state",
    )(row_valid, pair, col_mask, start_gain, start_in)
    row_state = lax.psum(row_state, "row")

    part = cols // CHUNKS
    tile = 16
    tiles = part // tile
    block = tile * (depth + 1)
    while block % 16 or (tiles * block) % (16 * size):
        block += 16
    bits = list(range(size.bit_length() - 1))
    full = jax.ShapeDtypeStruct(pair.shape, BF16)

    update_start = None
    normed_parts, column_states = [], []
    for chunk in range(CHUNKS):
        extra = [] if update_start is None else [update_start]
        pair_block = pl.BlockSpec((group, part, width), lambda g, c=chunk: (g, c, 0))
        update_start, normed = pl.pallas_call(
            start_kernel,
            grid=(rows // group,),
            in_specs=[
                pair_block,
                pl.BlockSpec((group, packed, width), lambda g: (g, 0, 0)),
                whole(start_gain),
                whole(start_head_gain),
                whole(start_in),
                whole(start_out),
                whole(end_gain),
            ]
            + [anywhere] * len(extra),
            out_specs=[pair_block, pl.BlockSpec((group, part, width), lambda g: (g, 0, 0))],
            out_shape=[full, jax.ShapeDtypeStruct((rows, part, width), BF16)],
            input_output_aliases={7: 0} if extra else {},
            compiler_params=params(),
            cost_estimate=cost(2e10),
            name="start_finish",
        )(pair, row_state, start_gain, start_head_gain, start_in, start_out, end_gain, *extra)
        normed_parts.append(normed)
        state = pl.pallas_call(
            functools.partial(column_state_kernel, chunk * part),
            grid=(tiles,),
            in_specs=[
                smem,
                pl.BlockSpec((rows, tile, width), lambda g: (0, g, 0)),
                whole(row_mask),
                whole(end_in),
            ],
            out_specs=pl.BlockSpec((1, block, width), lambda g: (g, 0, 0)),
            out_shape=jax.ShapeDtypeStruct((tiles, block, width), BF16),
            scratch_shapes=[pltpu.VMEM((rows * tile, width), F32)],
            compiler_params=params(),
            cost_estimate=cost(1e10),
            name="column_state",
        )(col_valid, normed, row_mask, end_in)
        order = bits if chunk % 2 == 0 else bits[1:] + bits[:1]
        state = exchange_sum(state.reshape(tiles * block, width), size, order)
        column_states.append(state.reshape(tiles, block, width))

    outs = []
    for chunk in range(CHUNKS):
        pair_block = pl.BlockSpec(
            (rows, tile, width), lambda g, c=chunk: (0, c * tiles + g, 0)
        )
        outs = pl.pallas_call(
            end_kernel,
            grid=(tiles,),
            in_specs=[
                pl.BlockSpec((rows, tile, width), lambda g: (0, g, 0)),
                pair_block,
                pair_block,
                pl.BlockSpec((1, block, width), lambda g: (g, 0, 0)),
                whole(end_head_gain),
                whole(end_in),
                whole(end_out),
                whole(trans_gain),
                whole(trans_in),
                whole(trans_out),
            ]
            + [anywhere] * len(outs),
            out_specs=[pair_block, pair_block],
            out_shape=[full, full],
            scratch_shapes=[pltpu.VMEM((rows * tile, width), F32)] * 2,
            input_output_aliases={10: 0, 11: 1} if outs else {},
            compiler_params=params(),
            cost_estimate=cost(5e10),
            name="end_finish",
        )(
            normed_parts[chunk],
            pair,
            update_start,
            column_states[chunk],
            end_head_gain,
            end_in,
            end_out,
            trans_gain,
            trans_in,
            trans_out,
            *outs,
        )
    return (update_start, outs[0], outs[1])


def solution(mesh):
    field = P(("groups", "col"), "row", None)
    in_specs = (field, P("groups")) + (P(),) * 11
    return jax.shard_map(
        functools.partial(shards, mesh.shape["col"]),
        mesh=mesh,
        in_specs=in_specs,
        out_specs=(field, field, field),
        check_vma=False,
    )
```

time: 764 us -> 384 us (0.50); the launches traced: 754 us -> 384 us
  Pallas kernels: 0 us -> 246 us
  waiting for transfers between devices: 307 us -> 98.5 us
  matrix products: 162 us -> 0 us
  other arithmetic: 159 us -> 5.03 us
  local copies, waits for them, and re-layouts: 107 us -> 3.35 us
  starting transfers between devices: 0.54 us -> 16.8 us
    psum x2 -> x1, waiting for transfers between devices: 307 us -> 22.3 us  [shards(): row_state = lax.psum(row_state, 'row')]
    pallas_call x0 -> x7, Pallas kernels: none -> 246 us  [the longest x2 93.5 us: shards(): pl.pallas_call(start_kernel, grid=(rows // group,), in_specs=[pair_block,...]
    dot_general x30 -> x0, matrix products: 162 us -> none  [the longest x10 34.3 us: transition(): lifted = jnp.dot(normed_block, trans_in, preferred_element_type=jnp.float32)]
    reduce_sum x26 -> x0, other arithmetic: 106 us -> none  [the longest x12 39.5 us: layer_norm(): variance = jnp.mean(centered * centered, axis=-1, keepdims=True)]
    ppermute x0 -> x12, waiting for transfers between devices: none -> 76.1 us  [the longest x6 54.2 us: exchange_sum(): got = lax.ppermute(sent, 'col', pairs)]
    reshape x5 -> x0, local copies, waits for them, and re-layouts: 72.4 us -> none  [the longest x2 33.7 us: finish(): attended = (numer / denom[..., None]).reshape(gating.shape)]
    convert_element_type x5 -> x7, other arithmetic: 46.3 us -> 1.38 us  [the longest x6 0.69 us: exchange_sum(): values = (kept.astype(F32) + got.astype(F32)).astype(BF16)]
    convert_element_type x2 -> x0, local copies, waits for them, and re-layouts: 20.2 us -> none  [the longest x1 10.4 us: shards(): feature(project[..., :width]).astype(jnp.bfloat16).reshape(head_shape)]
  transfers between devices with their start and end apart: 2 -> 13, of which waited for: 1 -> 9; matrix products, arithmetic and copies ran while one was open for 7% -> 1% of each run, Pallas kernels for 0% -> 27%
where the time goes in v1:
time: 384 us
  Pallas kernels  246 us (64%)
  waiting for transfers between devices  98.5 us (26%)
  starting transfers between devices  16.8 us (4%)
  between operations  14.3 us (4%)
  other arithmetic  5.03 us (1%)
    pallas_call x2, Pallas kernels, shards(): pl.pallas_call(start_kernel, grid=(rows // group,), in_specs=[pair_block,...  93.5 us
    pallas_call x2, Pallas kernels, shards(): pl.pallas_call(end_kernel, grid=(tiles,), in_specs=[pl.BlockSpec((rows, t...  91.7 us
    ppermute x6, waiting for transfers between devices, exchange_sum(): got = lax.ppermute(sent, 'col', pairs)  54.2 us
    pallas_call x1, Pallas kernels, shards(): pl.pallas_call(row_state_kernel, grid=(rows // group,), in_specs=[smem, p...  41.6 us
    psum x1, waiting for transfers between devices, shards(): row_state = lax.psum(row_state, 'row')  22.3 us
    ppermute x6, waiting for transfers between devices, exchange_sum(): got = lax.ppermute(values, 'col', pairs)  21.9 us
    pallas_call x2, Pallas kernels, shards(): pl.pallas_call(functools.partial(column_state_kernel, chunk * part), grid...  18.8 us
    ppermute x6, starting transfers between devices, exchange_sum(): got = lax.ppermute(sent, 'col', pairs)  8.74 us
  transfers between devices with their start and end apart: 13, of which 9 were waited for; matrix products, arithmetic and copies ran while one was open for 1% of the time, Pallas kernels for 27%

profile of v1, /device:TPU:0, one launch (start us, length us, event | category | flops | bytes accessed | tf_op | source)
XLA Modules:
  0.0 383.6 jit_solution(3196480910437377216)
XLA Ops:
  7.2 0.7 convert_element_type.57
  7.9 0.1 dynamic_slice.42.row_valid
  8.0 0.1 dynamic_slice.43.col_valid
  8.1 0.1 broadcast_in_dim.4.col_mask
  8.2 0.9 copy-done.3
  9.1 0.7 copy-done.9
  9.8 41.6 %row_state.1 = bf16[80,48,128]{2,1,0:T(8,128)(2,1)} custom-call(f32[80]{0:T(128)S(1)} %dynamic_slice.42.row_valid, bf16[80,320,128]{2,1,0:T(8,128)(2,1)} %pair.9, f32[320,128]{1,0:T(8,128)S(1)} %broadcast_in_dim.4.col_mask, f32[1,128]{1,0:T(1,128)S(1)} %bitcast.13, bf16[128,512]{1,0:T(8,128)(2,1)S(1)} %copy-done.3), custom_call_target="tpu_custom_call" | custom-call | flops 20000000000 | bytes 1048576 | tf_op jit(solution)/shard_map/row_state/pallas_call | solution.py:264
  51.4 22.3 %all-reduce.2.cloned.1.call-done.state = bf16[80,48,128]{2,1,0:T(8,128)(2,1)} async-done(((bf16[80,48,128]{2,1,0:T(8,128)(2,1)}), bf16[80,48,128]{2,1,0:T(8,128)(2,1)}) %all-reduce.2.cloned.1.call-update) | async-done | bytes 983056 | tf_op jit(solution)/shard_map/psum | solution.py:280
  73.8 1.2 copy-done
  75.0 46.8 %start_finish.2 = (bf16[80,320,128]{2,1,0:T(8,128)(2,1)}, bf16[80,160,128]{2,1,0:T(8,128)(2,1)}) custom-call(bf16[80,320,128]{2,1,0:T(8,128)(2,1)} %pair.9, bf16[80,48,128]{2,1,0:T(8,128)(2,1)S(1)} %copy-done, f32[1,128]{1,0:T(1,128)S(1)} %bitcast.14, f32[1,128]{1,0:T(1,128)S(1)} %bitcast.16, bf16[128,512]{1,0:T(8,128)(2,1)S(1)} %copy-done.4, ...), custom_call_target="tpu_custom_call" | custom-call | flops 20000000000 | bytes 1048576 | tf_op jit(solution)/shard_map/start_finish/pallas_call | solution.py:296
  121.8 0.1 broadcast_in_dim.5.row_mask
  121.9 9.4 %column_state.3 = bf16[10,576,128]{2,1,0:T(8,128)(2,1)S(1)} custom-call(f32[320]{0:T(512)S(1)} %dynamic_slice.43.col_valid, bf16[80,160,128]{2,1,0:T(8,128)(2,1)} %get-tuple-element.14.normed, f32[80,128]{1,0:T(8,128)S(1)} %broadcast_in_dim.5.row_mask, bf16[128,512]{1,0:T(8,128)(2,1)S(1)} %copy-done.5), custom_call_target="tpu_custom_call" | custom-call | flops 10000000000 | bytes 1048576 | tf_op jit(solution)/shard_map/column_state/pallas_call | solution.py:317
  131.3 0.1 constant_dynamic-slice_fusion.2
  131.4 1.8 collective-permute-start.6
  133.2 46.7 %start_finish.3 = (bf16[80,320,128]{2,1,0:T(8,128)(2,1)}, bf16[80,160,128]{2,1,0:T(8,128)(2,1)}) custom-call(bf16[80,320,128]{2,1,0:T(8,128)(2,1)} %pair.9, bf16[80,48,128]{2,1,0:T(8,128)(2,1)S(1)} %copy-done.1, f32[1,128]{1,0:T(1,128)S(1)} %bitcast.15, f32[1,128]{1,0:T(1,128)S(1)} %bitcast.17, ...), custom_call_target="tpu_custom_call", output_to_operand_aliasing={{0}: (7, {})} | custom-call | flops 20000000000 | bytes 1048576 | tf_op jit(solution)/shard_map/start_finish/pallas_call | solution.py:296
  179.9 9.4 %column_state.2 = bf16[10,576,128]{2,1,0:T(8,128)(2,1)S(1)} custom-call(f32[320]{0:T(512)S(1)} %dynamic_slice.43.col_valid, bf16[80,160,128]{2,1,0:T(8,128)(2,1)} %get-tuple-element.13.normed, f32[80,128]{1,0:T(8,128)S(1)} %broadcast_in_dim.5.row_mask, bf16[128,512]{1,0:T(8,128)(2,1)S(1)} %copy-done.5), custom_call_target="tpu_custom_call" | custom-call | flops 10000000000 | bytes 1048576 | tf_op jit(solution)/shard_map/column_state/pallas_call | solution.py:317
  189.3 0.1 constant_dynamic-slice_fusion.5
  189.4 1.6 collective-permute-start
  190.9 0.2 add_convert_fusion
  191.2 0.6 collective-permute-start.7
  191.8 17.0 %collective-permute-done = bf16[2880,128]{1,0:T(8,128)(2,1)S(1)} collective-permute-done((bf16[2880,128]{1,0:T(8,128)(2,1)S(1)}, bf16[2880,128]{1,0:T(8,128)(2,1)S(1)}, u32[]{:S(2)}, u32[]{:S(2)}) %collective-permute-start) | collective-permute-done | bytes 737312 | tf_op jit(solution)/shard_map/ppermute | solution.py:207
  208.8 0.2 add_convert_fusion.1
  209.0 6.7 %collective-permute-done.7 = bf16[1440,128]{1,0:T(8,128)(2,1)S(1)} collective-permute-done((bf16[1440,128]{1,0:T(8,128)(2,1)S(1)}, bf16[1440,128]{1,0:T(8,128)(2,1)S(1)}, u32[]{:S(2)}, u32[]{:S(2)}) %collective-permute-start.7) | collective-permute-done | bytes 368672 | tf_op jit(solution)/shard_map/ppermute | solution.py:207
  215.8 0.1 add_convert_fusion.2
  215.9 2.5 collective-permute-start.8
  218.4 0.6 collective-permute-start.1
  219.0 16.5 %collective-permute-done.8 = bf16[720,128]{1,0:T(8,128)(2,1)S(1)} collective-permute-done((bf16[720,128]{1,0:T(8,128)(2,1)S(1)}, bf16[720,128]{1,0:T(8,128)(2,1)S(1)}, u32[]{:S(2)}, u32[]{:S(2)}) %collective-permute-start.8) | collective-permute-done | bytes 184352 | tf_op jit(solution)/shard_map/ppermute | solution.py:207
  235.5 0.1 collective-permute-start.9
  235.6 11.7 %collective-permute-done.1 = bf16[1440,128]{1,0:T(8,128)(2,1)S(1)} collective-permute-done((bf16[1440,128]{1,0:T(8,128)(2,1)S(1)}, bf16[1440,128]{1,0:T(8,128)(2,1)S(1)}, u32[]{:S(2)}, u32[]{:S(2)}) %collective-permute-start.1) | collective-permute-done | bytes 368672 | tf_op jit(solution)/shard_map/ppermute | solution.py:207
  247.3 0.1 add_convert_fusion.3
  247.5 1.7 collective-permute-start.2
  249.2 1.0 collective-permute-done.9
  250.2 0.1 maximum_select_fusion.5
  250.3 0.6 collective-permute-start.10
  250.9 2.2 collective-permute-done.2
  253.1 1.7 collective-permute-start.3
  254.8 5.1 %collective-permute-done.10 = bf16[1440,128]{1,0:T(8,128)(2,1)S(1)} collective-permute-done((bf16[1440,128]{1,0:T(8,128)(2,1)S(1)}, bf16[1440,128]{1,0:T(8,128)(2,1)S(1)}, u32[]{:S(2)}, u32[]{:S(2)}) %collective-permute-start.10) | collective-permute-done | bytes 368672 | tf_op jit(solution)/shard_map/ppermute | solution.py:212
  259.9 0.2 maximum_select_fusion.3
  260.1 1.7 collective-permute-start.11
  261.8 0.1 maximum_select_fusion.4
  261.9 3.2 collective-permute-start.4
  265.1 15.9 %collective-permute-done.4 = bf16[1440,128]{1,0:T(8,128)(2,1)S(1)} collective-permute-done((bf16[1440,128]{1,0:T(8,128)(2,1)S(1)}, bf16[1440,128]{1,0:T(8,128)(2,1)S(1)}, u32[]{:S(2)}, u32[]{:S(2)}) %collective-permute-start.4) | collective-permute-done | bytes 368672 | tf_op jit(solution)/shard_map/ppermute | solution.py:212
  281.0 0.2 maximum_select_fusion.2
  281.2 0.7 collective-permute-start.5
  282.0 1.5 maximum_select_fusion.1
  283.5 45.8 %end_finish.2 = (bf16[80,320,128]{2,1,0:T(8,128)(2,1)}, bf16[80,320,128]{2,1,0:T(8,128)(2,1)}) custom-call(bf16[80,160,128]{2,1,0:T(8,128)(2,1)} %get-tuple-element.14.normed, bf16[80,320,128]{2,1,0:T(8,128)(2,1)} %pair.9, bf16[80,320,128]{2,1,0:T(8,128)(2,1)} %get-tuple-element.8.update_start, bf16[10,576,128]{2,1,0:T(8,128)(2,1)} %bitcast.25, ...), custom_call_target="tpu_custom_call" | custom-call | flops 49999998976 | bytes 1048576 | tf_op jit(solution)/shard_map/end_finish/pallas_call | solution.py:342
  329.4 1.5 maximum_select_fusion
  330.9 45.9 %end_finish.3 = (bf16[80,320,128]{2,1,0:T(8,128)(2,1)}, bf16[80,320,128]{2,1,0:T(8,128)(2,1)}) custom-call(bf16[80,160,128]{2,1,0:T(8,128)(2,1)} %get-tuple-element.13.normed, bf16[80,320,128]{2,1,0:T(8,128)(2,1)} %pair.9, bf16[80,320,128]{2,1,0:T(8,128)(2,1)} %get-tuple-element.8.update_start, ...), custom_call_target="tpu_custom_call", output_to_operand_aliasing={{0}: (10, {}), {1}: (11, {})} | custom-call | flops 49999998976 | bytes 1048576 | tf_op jit(solution)/shard_map/end_finish/pallas_call | solution.py:342
  (39 shorter events, 0.3 us)
Async XLA Ops:
  7.2 66.6 %all-reduce.2.cloned.1.call-start = ((), (), s32[]{:S(2)}) async-start(), calls=%async_computation | async-start | bytes 1966080 | tf_op jit(solution)/shard_map/psum | solution.py:280
  8.2 0.9 copy-start.3
  9.1 0.7 copy-start.9
  9.7 64.1 %copy-start.4 = (bf16[128,512]{1,0:T(8,128)(2,1)S(1)}, bf16[128,512]{1,0:T(8,128)(2,1)}, u32[]{:S(2)}) copy-start(bf16[128,512]{1,0:T(8,128)(2,1)} %w.9) | copy-start | bytes 393220
  9.7 64.1 %copy-start.7 = (bf16[128,128]{1,0:T(8,128)(2,1)S(1)}, bf16[128,128]{1,0:T(8,128)(2,1)}, u32[]{:S(2)}) copy-start(bf16[128,128]{1,0:T(8,128)(2,1)} %w_out.5) | copy-start | bytes 98308
  9.7 64.1 %copy-start.10 = (f32[128]{0:T(128)S(1)}, f32[128]{0:T(128)}, u32[]{:S(2)}) copy-start(f32[128]{0:T(128)} %param.15) | copy-start | bytes 1540
  9.7 64.1 %copy-start.11 = (f32[128]{0:T(128)S(1)}, f32[128]{0:T(128)}, u32[]{:S(2)}) copy-start(f32[128]{0:T(128)} %param.16) | copy-start | bytes 1540
  9.7 64.1 %copy-start.12 = (f32[128]{0:T(128)S(1)}, f32[128]{0:T(128)}, u32[]{:S(2)}) copy-start(f32[128]{0:T(128)} %param.19) | copy-start | bytes 1540
  73.8 1.2 copy-start
  75.0 46.9 %copy-start.5 = (bf16[128,512]{1,0:T(8,128)(2,1)S(1)}, bf16[128,512]{1,0:T(8,128)(2,1)}, u32[]{:S(2)}) copy-start(bf16[128,512]{1,0:T(8,128)(2,1)} %w.13) | copy-start | bytes 393220
  131.3 1.9 copy-start.1
  131.4 59.6 %collective-permute-start.6 = (bf16[2880,128]{1,0:T(8,128)(2,1)S(1)}, bf16[2880,128]{1,0:T(8,128)(2,1)S(1)}, u32[]{:S(2)}, u32[]{:S(2)}) collective-permute-start(bf16[2880,128]{1,0:T(8,128)(2,1)S(1)} %constant_dynamic-slice_fusion.2), channel_id=1, source_target_pairs={{0,1},{1,0},{2,3},{3,2},{4,5},{5,4},{6,7},{7,6},{8,9},{9,8},{10,11... | collective-permute-start | bytes 2211848 | tf_op jit(solution)/shard_map/ppermute | solution.py:207
  189.4 19.4 %collective-permute-start = (bf16[2880,128]{1,0:T(8,128)(2,1)S(1)}, bf16[2880,128]{1,0:T(8,128)(2,1)S(1)}, u32[]{:S(2)}, u32[]{:S(2)}) collective-permute-start(bf16[2880,128]{1,0:T(8,128)(2,1)S(1)} %constant_dynamic-slice_fusion.5), channel_id=1, source_target_pairs={{0,2},{1,3},{2,0},{3,1},{4,6},{5,7},{6,4},{7,5},{8,10},{9,11},{10,... | collective-permute-start | bytes 2211848 | tf_op jit(solution)/shard_map/ppermute | solution.py:207
  191.2 24.6 %collective-permute-start.7 = (bf16[1440,128]{1,0:T(8,128)(2,1)S(1)}, bf16[1440,128]{1,0:T(8,128)(2,1)S(1)}, u32[]{:S(2)}, u32[]{:S(2)}) collective-permute-start(bf16[1440,128]{1,0:T(8,128)(2,1)S(1)} %constant_dynamic-slice_fusion.1), channel_id=1, source_target_pairs={{0,2},{1,3},{2,0},{3,1},{4,6},{5,7},{6,4},{7,5},{8,10},{9,11},{10,... | collective-permute-start | bytes 1105928 | tf_op jit(solution)/shard_map/ppermute | solution.py:207
  215.9 19.6 %collective-permute-start.8 = (bf16[720,128]{1,0:T(8,128)(2,1)S(1)}, bf16[720,128]{1,0:T(8,128)(2,1)S(1)}, u32[]{:S(2)}, u32[]{:S(2)}) collective-permute-start(bf16[720,128]{1,0:T(8,128)(2,1)S(1)} %constant_dynamic-slice_fusion), channel_id=1, source_target_pairs={{0,4},{1,5},{2,6},{3,7},{4,0},{5,1},{6,2},{7,3},{8,12},{9,13},{10,... | collective-permute-start | bytes 552968 | tf_op jit(solution)/shard_map/ppermute | solution.py:207
  218.4 28.9 %collective-permute-start.1 = (bf16[1440,128]{1,0:T(8,128)(2,1)S(1)}, bf16[1440,128]{1,0:T(8,128)(2,1)S(1)}, u32[]{:S(2)}, u32[]{:S(2)}) collective-permute-start(bf16[1440,128]{1,0:T(8,128)(2,1)S(1)} %constant_dynamic-slice_fusion.4), channel_id=1, source_target_pairs={{0,4},{1,5},{2,6},{3,7},{4,0},{5,1},{6,2},{7,3},{8,12},{9,13},{10,... | collective-permute-start | bytes 1105928 | tf_op jit(solution)/shard_map/ppermute | solution.py:207
  235.5 14.7 %collective-permute-start.9 = (bf16[720,128]{1,0:T(8,128)(2,1)S(1)}, bf16[720,128]{1,0:T(8,128)(2,1)S(1)}, u32[]{:S(2)}, u32[]{:S(2)}) collective-permute-start(bf16[720,128]{1,0:T(8,128)(2,1)S(1)} %add_convert_fusion.4), channel_id=1, source_target_pairs={{0,4},{1,5},{2,6},{3,7},{4,0},{5,1},{6,2},{7,3},{8,12},{9,13},{10,... | collective-permute-start | bytes 552968 | tf_op jit(solution)/shard_map/ppermute | solution.py:212
  247.5 5.6 %collective-permute-start.2 = (bf16[720,128]{1,0:T(8,128)(2,1)S(1)}, bf16[720,128]{1,0:T(8,128)(2,1)S(1)}, u32[]{:S(2)}, u32[]{:S(2)}) collective-permute-start(bf16[720,128]{1,0:T(8,128)(2,1)S(1)} %constant_dynamic-slice_fusion.3), channel_id=1, source_target_pairs={{0,1},{1,0},{2,3},{3,2},{4,5},{5,4},{6,7},{7,6},{8,9},{9,8},{10,11... | collective-permute-start | bytes 552968 | tf_op jit(solution)/shard_map/ppermute | solution.py:207
  250.3 9.6 %collective-permute-start.10 = (bf16[1440,128]{1,0:T(8,128)(2,1)S(1)}, bf16[1440,128]{1,0:T(8,128)(2,1)S(1)}, u32[]{:S(2)}, u32[]{:S(2)}) collective-permute-start(bf16[1440,128]{1,0:T(8,128)(2,1)S(1)} %maximum_select_fusion.5), channel_id=1, source_target_pairs={{0,2},{1,3},{2,0},{3,1},{4,6},{5,7},{6,4},{7,5},{8,10},{9,11},{10,... | collective-permute-start | bytes 1105928 | tf_op jit(solution)/shard_map/ppermute | solution.py:212
  253.1 8.7 %collective-permute-start.3 = (bf16[720,128]{1,0:T(8,128)(2,1)S(1)}, bf16[720,128]{1,0:T(8,128)(2,1)S(1)}, u32[]{:S(2)}, u32[]{:S(2)}) collective-permute-start(bf16[720,128]{1,0:T(8,128)(2,1)S(1)} %add_convert_fusion.5), channel_id=1, source_target_pairs={{0,1},{1,0},{2,3},{3,2},{4,5},{5,4},{6,7},{7,6},{8,9},{9,8},{10,11... | collective-permute-start | bytes 552968 | tf_op jit(solution)/shard_map/ppermute | solution.py:212
  260.1 21.9 %collective-permute-start.11 = (bf16[2880,128]{1,0:T(8,128)(2,1)S(1)}, bf16[2880,128]{1,0:T(8,128)(2,1)S(1)}, u32[]{:S(2)}, u32[]{:S(2)}) collective-permute-start(bf16[2880,128]{1,0:T(8,128)(2,1)S(1)} %maximum_select_fusion.3), channel_id=1, source_target_pairs={{0,1},{1,0},{2,3},{3,2},{4,5},{5,4},{6,7},{7,6},{8,9},{9,8},{10,11... | collective-permute-start | bytes 2211848 | tf_op jit(solution)/shard_map/ppermute | solution.py:212
  261.9 19.1 %collective-permute-start.4 = (bf16[1440,128]{1,0:T(8,128)(2,1)S(1)}, bf16[1440,128]{1,0:T(8,128)(2,1)S(1)}, u32[]{:S(2)}, u32[]{:S(2)}) collective-permute-start(bf16[1440,128]{1,0:T(8,128)(2,1)S(1)} %maximum_select_fusion.4), channel_id=1, source_target_pairs={{0,4},{1,5},{2,6},{3,7},{4,0},{5,1},{6,2},{7,3},{8,12},{9,13},{10,... | collective-permute-start | bytes 1105928 | tf_op jit(solution)/shard_map/ppermute | solution.py:212
  281.2 2.3 copy-start.2
  281.2 2.3 copy-start.6
  281.2 2.3 copy-start.8
  281.2 2.3 copy-start.13
  281.2 2.3 copy-start.14
  281.2 48.1 %collective-permute-start.5 = (bf16[2880,128]{1,0:T(8,128)(2,1)S(1)}, bf16[2880,128]{1,0:T(8,128)(2,1)S(1)}, u32[]{:S(2)}, u32[]{:S(2)}) collective-permute-start(bf16[2880,128]{1,0:T(8,128)(2,1)S(1)} %maximum_select_fusion.2), channel_id=1, source_target_pairs={{0,2},{1,3},{2,0},{3,1},{4,6},{5,7},{6,4},{7,5},{8,10},{9,11},{10,... | collective-permute-start | bytes 2211848 | tf_op jit(solution)/shard_map/ppermute | solution.py:212
Sparse Core Ops, SparseCore 0:
  51.5 22.1 all-reduce.1
